TPU v7x, 512 devices: a whole 4x4x16 slice. The times are simulated.
512 devices in a mesh: dc: 128 (over y, z, core), tp: 4 (over x).
Axes of the slice: x: 4, y: 4, z: 16, core: 2. Of those that a mesh axis runs over, the one named last changes fastest.
Arguments:
- query_pre: bfloat16 [256, 128, 2048], P(None, 'dc', 'tp'), may hold values from -40 to 40
- key_pre: bfloat16 [256, 128, 512], P(None, 'dc', 'tp'), may hold values from -40 to 40
- values: bfloat16 [256, 128, 512], P(None, 'dc', 'tp'), may hold values from -6 to 6
- grad_out: bfloat16 [256, 128, 2048], P(None, 'dc', 'tp'), may hold values from -40 to 40
- query_gain: bfloat16 [128], replicated, may hold values from 1 to 8
- key_gain: bfloat16 [128], replicated, may hold values from 1 to 8
- doc_units: int32 [128], replicated, may hold values from 1 to 3, as said below
Outputs:
- grad_query: bfloat16 [256, 128, 2048], P(None, 'dc', 'tp')
- grad_key: bfloat16 [256, 128, 512], P(None, 'dc', 'tp')
- grad_values: bfloat16 [256, 128, 512], P(None, 'dc', 'tp')
- grad_query_gain: float32 [128], replicated
- grad_key_gain: float32 [128], replicated
Inputs may be any that keep to these rules, and one draw needn't show every extreme that they name: Document i holds doc_units[i] * 128 tokens; the lengths sum to 256; the first two documents hold 1 and 3 units.
All inputs are finite; a program needn't handle non-finite values.
Results may differ from a plain program's by a relative error of at most 0.035.
The roundings to bfloat16 on the way count: a program that leaves them out, or rounds other values in their place, can miss the bound.
Values may be sent and summed in bfloat16 or wider, within the bound.
A program may use at most 64 MiB of HBM per device.

v0:
```python
import math

import jax
import jax.numpy as jnp
from jax import lax
from jax.experimental import pallas as pl
from jax.experimental.pallas import tpu as pltpu
from jax.sharding import PartitionSpec as P

HEADS = 4
DIM = 128
UNIT = 128
EPS = 1e-06
THETA = 1000000.0
SCALE = 1.0 / math.sqrt(DIM)
MASKED = -1e30

NZ = 16
NJ = 8
NX = 4
ROWS = NZ * NJ * 2

K_AT, V_AT, Q_AT, G_AT, FWD = 0, 128, 256, 768, 1280
DQ_AT, DK_AT, DV_AT, BACK = 0, 512, 640, 768
PIECE = 2
PIECES = HEADS // PIECE
WIDE = PIECE * DIM

MESH = pl.DeviceIdType.MESH
F32 = jnp.float32
BF16 = jnp.bfloat16


def dot(a, b, dims):
    return lax.dot_general(a, b, (dims, ((), ())), preferred_element_type=F32)


def swap_halves(x):
    return pltpu.roll(x, DIM // 2, 1)


def kernel(
    q_in, k_in, v_in, g_in, qgain_ref, kgain_ref, docs_ref,
    dq_out, dk_out, dv_out, gain_out,
    r1, s2, r2, s3, r3, s4, kwin, vwin, halo_s, halo_r,
    qrot, qhat, qinv, khat, kinv, prob, dkacc, dvacc, perm, cosw, sinw, gpart,
    gx, gj, gz,
    sem1, sem2, sem3, sem4, semh, semg, send,
):
    me = lax.axis_index("dc")
    x = lax.axis_index("tp")
    y = me // 32
    z = lax.rem(me, 32) // 2
    c = lax.rem(me, 2)
    j = y * 2 + c
    p = z * NJ + j

    def at(yy, zz, cc):
        return (yy * 32 + zz * 2 + cc, x)

    def z_peer(i):
        k = i // 2 + 1
        other = lax.rem(jnp.where(lax.rem(i, 2) == 0, z + k, z + NZ - k), NZ)
        return other, at(y, other, c)

    def j_peer(i):
        other = lax.rem(j + 1 + i, NJ)
        return other, at(other // 2, z, lax.rem(other, 2))

    def x_peer(i):
        other = lax.rem(x + 1 + i, NX)
        return other, (me, other)

    def owner(pp):
        pp = lax.rem(pp + ROWS // 2, ROWS // 2)
        jj = lax.rem(pp, NJ)
        return at(jj // 2, pp // NJ, lax.rem(jj, 2))

    def each(count, body):
        def step(i, carry):
            body(i)
            return carry

        lax.fori_loop(0, count, step, 0)

    def remote(src, dst, send_sem, recv_sem, device):
        pltpu.make_async_remote_copy(
            src_ref=src, dst_ref=dst, send_sem=send_sem, recv_sem=recv_sem,
            device_id=device, device_id_type=MESH,
        ).start()

    def wait(ref, sem):
        pltpu.make_async_copy(ref, ref, sem).wait()

    barrier = pltpu.get_barrier_semaphore()

    def greet(device):
        pl.semaphore_signal(barrier, inc=1, device_id=device, device_id_type=MESH)

    each(NZ - 1, lambda i: greet(z_peer(i)[1]))
    each(NJ - 1, lambda i: greet(j_peer(i)[1]))
    each(NX - 1, lambda i: greet(x_peer(i)[1]))
    greet(owner(p + 1))
    greet(owner(p - 1))
    pl.semaphore_wait(barrier, NZ - 1 + NJ - 1 + NX - 1 + 2)

    sources = [(k_in, 0, K_AT, DIM), (v_in, 0, V_AT, DIM)]
    sources += [(q_in, n * WIDE, Q_AT + n * WIDE, WIDE) for n in range(PIECES)]
    sources += [(g_in, n * WIDE, G_AT + n * WIDE, WIDE) for n in range(PIECES)]
    for n, (ref, start, lane, width) in enumerate(sources):
        here = r1.at[pl.ds(pl.multiple_of(z * 16, 16), 16), pl.ds(lane, width)]

        def block(other, ref=ref, start=start, width=width):
            return ref.at[pl.ds(pl.multiple_of(other * 16, 16), 16), pl.ds(start, width)]

        def go(i, block=block, here=here, n=n):
            other, device = z_peer(i)
            remote(block(other), here, send.at[0], sem1.at[n], device)

        pltpu.make_async_copy(block(z), here, sem1.at[n]).start()
        each(NZ - 1, go)

    row = lax.broadcasted_iota(jnp.int32, (ROWS, ROWS), 0)
    col = lax.broadcasted_iota(jnp.int32, (ROWS, ROWS), 1)
    perm[...] = jnp.where((row % 16) * 16 + row // 16 == col, 1.0, 0.0).astype(BF16)

    lens = jnp.broadcast_to(docs_ref[...].astype(F32), (UNIT, UNIT))
    doc = lax.broadcasted_iota(jnp.int32, (UNIT, UNIT), 0)
    before = lax.broadcasted_iota(jnp.int32, (UNIT, UNIT), 1)
    starts = jnp.sum(jnp.where(before < doc, lens, 0.0), axis=1, keepdims=True)
    unit = [(2 * p + u).astype(F32) for u in range(2)]
    first = [
        jnp.max(jnp.where(starts <= unit[u], starts, 0.0), axis=0, keepdims=True)
        for u in range(2)
    ]

    def token(index):
        jj = index // 16
        return (jj // 2) * 32 + (index % 16) * 2 + jj % 2

    lane = lax.broadcasted_iota(jnp.int32, (UNIT, DIM), 1)
    place = token(lax.broadcasted_iota(jnp.int32, (UNIT, DIM), 0))
    half = DIM // 2
    freq = jnp.exp((lane % half).astype(F32) * (-2.0 * math.log(THETA) / DIM))
    for u in range(2):
        angle = (place.astype(F32) + (unit[u] - first[u]) * UNIT) * freq
        cosw[u * UNIT : (u + 1) * UNIT] = jnp.cos(angle)
        sinw[u * UNIT : (u + 1) * UNIT] = jnp.where(lane < half, -1.0, 1.0) * jnp.sin(angle)

    causal = jnp.where(
        token(lax.broadcasted_iota(jnp.int32, (UNIT, UNIT), 0))
        <= token(lax.broadcasted_iota(jnp.int32, (UNIT, UNIT), 1)),
        0.0,
        MASKED,
    )
    causal = jnp.concatenate([causal] * PIECE, axis=1)
    seen = [
        [jnp.where(first[u] <= unit[u] - back, 0.0, MASKED) for back in (2, 1)]
        for u in range(2)
    ]
    qgain = qgain_ref[...].astype(F32)
    kgain = kgain_ref[...].astype(F32)

    def turn(a):
        return a * cosw[...] + swap_halves(a) * sinw[...]

    def turn_back(a):
        return a * cosw[...] - swap_halves(a) * sinw[...]

    def norm(raw):
        wide = raw.astype(F32)
        inv = lax.rsqrt(jnp.mean(wide * wide, axis=1, keepdims=True) + EPS)
        return wide * inv, inv

    def norm_back(grad, hat, inv, gain):
        turned = turn_back(grad)
        scaled = turned * gain
        out = inv * (scaled - hat * jnp.mean(scaled * hat, axis=1, keepdims=True))
        return out.astype(BF16), jnp.sum(turned * hat, axis=0, keepdims=True)

    def spread(n):
        _, _, lane, width = sources[n]
        lanes = pl.ds(lane, width)
        wait(r1.at[:, lanes], sem1.at[n])
        moved = dot(perm[...], r1[:, lanes], ((1,), (0,))).astype(BF16)
        s2[:, :, lanes] = moved.reshape(16, 16, width)
        here = r2.at[:, pl.ds(pl.multiple_of(j * 16, 16), 16), lanes]

        def go(i):
            other, device = j_peer(i)
            remote(s2.at[pl.ds(other * 2, 2), :, lanes], here, send.at[1], sem2.at[n], device)

        pltpu.make_async_copy(s2.at[pl.ds(j * 2, 2), :, lanes], here, sem2.at[n]).start()
        each(NJ - 1, go)

    def arrived(n):
        _, _, lane, width = sources[n]
        wait(r2.at[:, :, pl.ds(lane, width)], sem2.at[n])

    def give_back(n, lane, width):
        lanes = pl.ds(lane, width)
        here = r3.at[pl.ds(j * 2, 2), :, lanes]

        def block(other):
            return s3.at[:, pl.ds(pl.multiple_of(other * 16, 16), 16), lanes]

        def go(i):
            other, device = j_peer(i)
            remote(block(other), here, send.at[2], sem3.at[n], device)

        pltpu.make_async_copy(block(j), here, sem3.at[n]).start()
        each(NJ - 1, go)

    def send_home(n, lane, width, out, start):
        lanes = pl.ds(lane, width)
        wait(r3.at[:, :, lanes], sem3.at[n])
        moved = dot(perm[...], r3[:, :, lanes].reshape(ROWS, width), ((1,), (0,)))
        s4[:, lanes] = moved.astype(BF16)
        here = out.at[pl.ds(pl.multiple_of(z * 16, 16), 16), pl.ds(start, width)]

        def block(other):
            return s4.at[pl.ds(pl.multiple_of(other * 16, 16), 16), lanes]

        def go(i):
            other, device = z_peer(i)
            remote(block(other), here, send.at[3], sem4.at[n], device)

        pltpu.make_async_copy(block(z), here, sem4.at[n]).start()
        each(NZ - 1, go)

    spread(0)
    spread(1)
    arrived(0)
    hat, inv = norm(r2[:, :, K_AT : K_AT + DIM].reshape(2 * UNIT, DIM))
    khat[...] = hat
    kinv[...] = inv
    kwin[2 * UNIT :] = turn(hat * kgain).astype(BF16)
    following = owner(p + 1)
    preceding = owner(p - 1)
    remote(kwin.at[pl.ds(2 * UNIT, 2 * UNIT)], kwin.at[pl.ds(0, 2 * UNIT)], send.at[4], semh.at[0], following)
    arrived(1)
    vwin[2 * UNIT :] = r2[:, :, V_AT : V_AT + DIM].reshape(2 * UNIT, DIM)
    remote(vwin.at[pl.ds(2 * UNIT, 2 * UNIT)], vwin.at[pl.ds(0, 2 * UNIT)], send.at[5], semh.at[1], following)

    def window(u):
        return slice(u * UNIT, (u + 3) * UNIT)

    def heads(n, u):
        return slice(n * WIDE, (n + 1) * WIDE)

    dkacc[...] = jnp.zeros_like(dkacc)
    dvacc[...] = jnp.zeros_like(dvacc)

    def scores(n):
        arrived(2 + n)
        for i in range(PIECE):
            h = n * PIECE + i
            raw = r2[:, :, Q_AT + h * DIM : Q_AT + (h + 1) * DIM].reshape(2 * UNIT, DIM)
            hat, inv = norm(raw)
            qhat[h] = hat
            qinv[h] = inv
            rot = turn(hat * qgain).astype(BF16)
            for u in range(2):
                qrot[u, h * UNIT : (h + 1) * UNIT] = rot[u * UNIT : (u + 1) * UNIT]
        if n == 0:
            wait(kwin.at[pl.ds(0, 2 * UNIT)], semh.at[0])
        for u in range(2):
            s = dot(kwin[window(u)], qrot[u, heads(n, u)], ((1,), (1,))) * SCALE
            s = jnp.concatenate(
                [
                    s[:UNIT] + seen[u][0],
                    s[UNIT : 2 * UNIT] + seen[u][1],
                    s[2 * UNIT :] + causal,
                ],
                axis=0,
            )
            e = jnp.exp(s - jnp.max(s, axis=0, keepdims=True))
            prob[u, n] = e * (1.0 / jnp.sum(e, axis=0, keepdims=True))

    def gradients(n):
        arrived(2 + PIECES + n)
        if n == 0:
            wait(vwin.at[pl.ds(0, 2 * UNIT)], semh.at[1])
        grads = [[None] * PIECE for _ in range(2)]
        for u in range(2):
            lanes = [G_AT + (n * PIECE + i) * DIM for i in range(PIECE)]
            g = jnp.concatenate([r2[u, :, a : a + DIM] for a in lanes], axis=0)
            att = prob[u, n]
            low = att.astype(BF16)
            datt = dot(vwin[window(u)], g, ((1,), (1,)))
            delta = jnp.sum(low.astype(F32) * datt, axis=0, keepdims=True)
            ds = (att * (datt - delta)).astype(BF16)
            dvacc[window(u)] += dot(low, g, ((1,), (0,)))
            dkacc[window(u)] += dot(ds, qrot[u, heads(n, u)], ((1,), (0,)))
            dq = (dot(ds, kwin[window(u)], ((0,), (0,))) * SCALE).astype(BF16).astype(F32)
            for i in range(PIECE):
                grads[u][i] = dq[i * UNIT : (i + 1) * UNIT]
        total = None
        for i in range(PIECE):
            h = n * PIECE + i
            grad = jnp.concatenate([grads[0][i], grads[1][i]], axis=0)
            out, part = norm_back(grad, qhat[h], qinv[h], qgain)
            s3[:, :, DQ_AT + h * DIM : DQ_AT + (h + 1) * DIM] = out.reshape(2, UNIT, DIM)
            total = part if total is None else total + part
        return total

    for n in range(PIECES):
        spread(2 + n)
        scores(n)

    qpart = None
    for n in range(PIECES):
        spread(2 + PIECES + n)
        if n > 0:
            send_home(n - 1, DQ_AT + (n - 1) * WIDE, WIDE, dq_out, (n - 1) * WIDE)
        part = gradients(n)
        qpart = part if qpart is None else qpart + part
        if n == PIECES - 1:
            halo_s[0] = dvacc[: 2 * UNIT].astype(BF16)
            halo_s[1] = (dkacc[: 2 * UNIT] * SCALE).astype(BF16)
            remote(halo_s, halo_r, send.at[6], semh.at[2], preceding)
        give_back(n, DQ_AT + n * WIDE, WIDE)
    wait(halo_r, semh.at[2])
    dv = dvacc[2 * UNIT :] + halo_r[0].astype(F32)
    s3[:, :, DV_AT:] = dv.astype(BF16).reshape(2, UNIT, DIM)
    give_back(PIECES, DV_AT, DIM)
    dk = dkacc[2 * UNIT :] * SCALE + halo_r[1].astype(F32)
    out, kpart = norm_back(dk.astype(BF16).astype(F32), khat[...], kinv[...], kgain)
    s3[:, :, DK_AT:DV_AT] = out.reshape(2, UNIT, DIM)
    give_back(PIECES + 1, DK_AT, DIM)

    which = lax.broadcasted_iota(jnp.int32, (8, DIM), 0)

    def share(stage, value, slots, mine, count, peer):
        gpart[stage] = value
        slots[mine] = value

        def go(i):
            remote(gpart.at[stage], slots.at[mine], send.at[7 + stage], semg.at[stage], peer(i)[1])

        each(count - 1, go)

    def total(stage, slots, count):
        wait(slots.at[pl.ds(0, count - 1)], semg.at[stage])
        return jnp.sum(slots[...], axis=0)

    own = jnp.where(which == 0, qpart, jnp.where(which == 1, kpart, 0.0))
    share(0, own, gx, x, NX, x_peer)
    last = PIECES - 1
    send_home(last, DQ_AT + last * WIDE, WIDE, dq_out, last * WIDE)
    share(1, total(0, gx, NX), gj, j, NJ, j_peer)
    send_home(PIECES, DV_AT, DIM, dv_out, 0)
    send_home(PIECES + 1, DK_AT, DIM, dk_out, 0)
    share(2, total(1, gj, NJ), gz, z, NZ, z_peer)
    gain_out[...] = total(2, gz, NZ)

    for n in range(PIECES):
        wait(dq_out.at[:, pl.ds(n * WIDE, WIDE)], sem4.at[n])
    wait(dv_out, sem4.at[PIECES])
    wait(dk_out, sem4.at[PIECES + 1])

    wait(r1.at[pl.ds(0, ROWS - 16)], send.at[0])
    wait(s2.at[pl.ds(0, 16 - 2)], send.at[1])
    wait(s3.at[:, pl.ds(0, UNIT - 16)], send.at[2])
    wait(s4.at[pl.ds(0, ROWS - 16)], send.at[3])
    wait(kwin.at[pl.ds(0, 2 * UNIT)], send.at[4])
    wait(vwin.at[pl.ds(0, 2 * UNIT)], send.at[5])
    wait(halo_s, send.at[6])
    wait(gx.at[pl.ds(0, NX - 1)], send.at[7])
    wait(gj.at[pl.ds(0, NJ - 1)], send.at[8])
    wait(gz.at[pl.ds(0, NZ - 1)], send.at[9])


def local(query_pre, key_pre, values, grad_out, query_gain, key_gain, doc_units):
    any_spec = pl.BlockSpec(memory_space=pl.ANY)
    vmem = pl.BlockSpec(memory_space=pltpu.VMEM)
    dma = pltpu.SemaphoreType.DMA
    dq, dk, dv, gains = pl.pallas_call(
        kernel,
        out_shape=[
            jax.ShapeDtypeStruct((ROWS, HEADS * DIM), BF16),
            jax.ShapeDtypeStruct((ROWS, DIM), BF16),
            jax.ShapeDtypeStruct((ROWS, DIM), BF16),
            jax.ShapeDtypeStruct((8, DIM), F32),
        ],
        in_specs=[any_spec] * 4 + [vmem] * 3,
        out_specs=[vmem] * 4,
        scratch_shapes=[
            pltpu.VMEM((ROWS, FWD), BF16),
            pltpu.VMEM((16, 16, FWD), BF16),
            pltpu.VMEM((2, UNIT, FWD), BF16),
            pltpu.VMEM((2, UNIT, BACK), BF16),
            pltpu.VMEM((16, 16, BACK), BF16),
            pltpu.VMEM((ROWS, BACK), BF16),
            pltpu.VMEM((4 * UNIT, DIM), BF16),
            pltpu.VMEM((4 * UNIT, DIM), BF16),
            pltpu.VMEM((2, 2 * UNIT, DIM), BF16),
            pltpu.VMEM((2, 2 * UNIT, DIM), BF16),
            pltpu.VMEM((2, HEADS * UNIT, DIM), BF16),
            pltpu.VMEM((HEADS, 2 * UNIT, DIM), F32),
            pltpu.VMEM((HEADS, 2 * UNIT, 1), F32),
            pltpu.VMEM((2 * UNIT, DIM), F32),
            pltpu.VMEM((2 * UNIT, 1), F32),
            pltpu.VMEM((2, PIECES, 3 * UNIT, WIDE), F32),
            pltpu.VMEM((4 * UNIT, DIM), F32),
            pltpu.VMEM((4 * UNIT, DIM), F32),
            pltpu.VMEM((ROWS, ROWS), BF16),
            pltpu.VMEM((2 * UNIT, DIM), F32),
            pltpu.VMEM((2 * UNIT, DIM), F32),
            pltpu.VMEM((3, 8, DIM), F32),
            pltpu.VMEM((NX, 8, DIM), F32),
            pltpu.VMEM((NJ, 8, DIM), F32),
            pltpu.VMEM((NZ, 8, DIM), F32),
            dma((2 + 2 * PIECES,)),
            dma((2 + 2 * PIECES,)),
            dma((2 + PIECES,)),
            dma((2 + PIECES,)),
            dma((3,)),
            dma((3,)),
            dma((10,)),
        ],
        compiler_params=pltpu.CompilerParams(
            collective_id=0, has_side_effects=True, vmem_limit_bytes=40 * 1024 * 1024
        ),
        cost_estimate=pl.CostEstimate(
            flops=1_300_000_000, bytes_accessed=4_000_000, transcendentals=1_000_000
        ),
    )(
        query_pre[:, 0, :],
        key_pre[:, 0, :],
        values[:, 0, :],
        grad_out[:, 0, :],
        query_gain.reshape(1, DIM),
        key_gain.reshape(1, DIM),
        doc_units.reshape(1, UNIT),
    )
    return dq[:, None, :], dk[:, None, :], dv[:, None, :], gains[0], gains[1]


def solution(mesh):
    token = P(None, "dc", "tp")
    return jax.shard_map(
        local,
        mesh=mesh,
        in_specs=(token, token, token, token, P(), P(), P()),
        out_specs=(token, token, token, P(), P()),
        check_vma=False,
    )
```

profile of v0, /device:TPU:1, one launch (start us, length us, event | category | flops | bytes accessed | tf_op | source)
XLA Modules:
  0.0 98.3 jit_solution(16094961302143774682)
XLA Ops:
  0.6 0.0 copy-start.4
  0.6 0.0 copy-start.5
  0.7 0.0 copy-start.6
  0.7 0.6 copy-done.4
  1.3 0.0 copy-done.5
  1.3 0.0 copy-done.6
  1.3 0.0 copy-start
  1.3 0.9 copy-done
  2.3 0.0 copy-start.1
  2.3 0.9 copy-done.1
  3.2 0.0 copy-start.2
  3.2 0.8 copy-done.2
  4.1 0.0 copy-start.3
  4.1 0.8 copy-done.3
  4.9 91.0 %shard_map.110 = (bf16[256,512]{1,0:T(8,128)(2,1)S(1)}, bf16[256,128]{1,0:T(8,128)(2,1)S(1)}, bf16[256,128]{1,0:T(8,128)(2,1)S(1)}, f32[8,128]{1,0:T(8,128)S(1)}) custom-call(bf16[256,512]{1,0:T(8,128)(2,1)S(1)} %bitcast.17, bf16[256,128]{1,0:T(8,128)(2,1)S(1)} %bitcast.19, bf16[256,128]{1,0:T(8,128)(2,1)S(1)} %bitcast.20, bf16[256,512]{1,0:T(8,128)(2,1)S(1)} %bitcast.18, ...), custom_call_target="tpu_custom_call" | custom-call | flops 1300000000 | bytes 4000000 | tf_op jit(solution)/shard_map/pallas_call | solution.py:378
  95.9 0.5 slice_bitcast_fusion
  96.4 0.7 copy.15
  97.1 0.6 copy.16
  97.7 0.6 copy.17
Async XLA Ops:
  0.6 0.7 copy-start.4
  0.6 0.7 copy-start.5
  0.7 0.7 copy-start.6
  1.3 0.9 copy-start
  2.3 0.9 copy-start.1
  3.2 0.8 copy-start.2
  4.1 0.8 copy-start.3
where the time goes:
time: 98.6 us; the launch traced here: 98.3 us
  Pallas kernels  91 us (92%)
  local copies, waits for them, and re-layouts  6.72 us (7%)
    pallas_call x1, Pallas kernels, local(): pl.pallas_call(kernel, out_shape=[jax.ShapeDtypeStruct((ROWS, HEADS * DIM...  91 us
    unnamed x17, local copies, waits for them, and re-layouts  6.2 us

commit v1 on v0

v1 whole, which is shorter than its diff:
```python
import math

import jax
import jax.numpy as jnp
from jax import lax
from jax.experimental import pallas as pl
from jax.experimental.pallas import tpu as pltpu
from jax.sharding import PartitionSpec as P

HEADS = 4
DIM = 128
UNIT = 128
EPS = 1e-06
THETA = 1000000.0
SCALE = 1.0 / math.sqrt(DIM)
MASKED = -1e30

NZ = 16
NJ = 8
NX = 4
AHEAD = 3
ROWS = NZ * NJ * 2

K_AT, V_AT, Q_AT, G_AT, FWD = 0, 128, 256, 768, 1280
DQ_AT, DK_AT, DV_AT, BACK = 0, 512, 640, 768

MESH = pl.DeviceIdType.MESH
F32 = jnp.float32
BF16 = jnp.bfloat16


def dot(a, b, dims):
    return lax.dot_general(a, b, (dims, ((), ())), preferred_element_type=F32)


def swap_halves(x):
    return pltpu.roll(x, DIM // 2, 1)


def kernel(
    q_in, k_in, v_in, g_in, qgain_in, kgain_in, docs_in,
    back_out, gain_out,
    qgain_ref, kgain_ref, docs_ref,
    r1, s2, r2, s3, r3, s4, kwin, vwin, halo_s, halo_r,
    qrot, qhat, qinv, khat, kinv, prob, dkacc, dvacc, perm, cosw, sinw, gpart,
    gx, gj, gz,
    sem1, sem2, sem3, sem4, semh, semg, send, small,
):
    me = lax.axis_index("dc")
    x = lax.axis_index("tp")
    y = me // 32
    z = lax.rem(me, 32) // 2
    c = lax.rem(me, 2)
    j = y * 2 + c
    p = z * NJ + j

    def at(yy, zz, cc):
        return (yy * 32 + zz * 2 + cc, x)

    def z_peer(i):
        i = NZ - 2 - i
        k = i // 2 + 1
        other = jnp.where((i & 1) == 0, z + k, z + NZ - k) & (NZ - 1)
        return other, at(y, other, c)

    def j_peer(i):
        other = (j + 1 + i) & (NJ - 1)
        return other, at(other // 2, z, other & 1)

    def x_peer(i):
        other = (x + 1 + i) & (NX - 1)
        return other, (me, other)

    def owner(pp):
        pp = (pp + ROWS // 2) & (ROWS // 2 - 1)
        jj = pp & (NJ - 1)
        return at(jj // 2, pp // NJ, jj & 1)

    def each(count, body):
        def step(i, carry):
            body(i)
            return carry

        lax.fori_loop(0, count, step, 0)

    def remote(src, dst, send_sem, recv_sem, device):
        pltpu.make_async_remote_copy(
            src_ref=src, dst_ref=dst, send_sem=send_sem, recv_sem=recv_sem,
            device_id=device, device_id_type=MESH,
        ).start()

    def wait(ref, sem):
        pltpu.make_async_copy(ref, ref, sem).wait()

    for n, (src, dst) in enumerate(
        ((qgain_in, qgain_ref), (kgain_in, kgain_ref), (docs_in, docs_ref))
    ):
        pltpu.make_async_copy(src, dst, small.at[n]).start()
    barrier = pltpu.get_barrier_semaphore()

    def greet(device):
        pl.semaphore_signal(barrier, inc=1, device_id=device, device_id_type=MESH)

    each(NZ - 1, lambda i: greet(z_peer(i)[1]))
    each(NJ - 1, lambda i: greet(j_peer(i)[1]))
    each(NX - 1, lambda i: greet(x_peer(i)[1]))
    greet(owner(p + 1))
    greet(owner(p - 1))
    pl.semaphore_wait(barrier, NZ - 1 + NJ - 1 + NX - 1 + 2)

    sources = [(k_in, 0, K_AT, DIM), (v_in, 0, V_AT, DIM)]
    sources += [(q_in, h * DIM, Q_AT + h * DIM, DIM) for h in range(HEADS)]
    sources += [(g_in, h * DIM, G_AT + h * DIM, DIM) for h in range(HEADS)]

    def depart(n):
        ref, start, lane, width = sources[n]
        here = r1.at[pl.ds(pl.multiple_of(z * 16, 16), 16), pl.ds(lane, width)]

        def block(other):
            return ref.at[pl.ds(pl.multiple_of(other * 16, 16), 16), pl.ds(start, width)]

        def go(i):
            other, device = z_peer(i)
            remote(block(other), here, send.at[0], sem1.at[n], device)

        pltpu.make_async_copy(block(z), here, sem1.at[n]).start()
        each(NZ - 1, go)

    for n in range(AHEAD):
        depart(n)

    row = lax.broadcasted_iota(jnp.int32, (ROWS, ROWS), 0)
    col = lax.broadcasted_iota(jnp.int32, (ROWS, ROWS), 1)
    perm[...] = jnp.where((row % 16) * 16 + row // 16 == col, 1.0, 0.0).astype(BF16)

    wait(qgain_ref, small.at[0])
    wait(kgain_ref, small.at[1])
    wait(docs_ref, small.at[2])

    lens = jnp.broadcast_to(docs_ref[...].astype(F32), (UNIT, UNIT))
    doc = lax.broadcasted_iota(jnp.int32, (UNIT, UNIT), 0)
    before = lax.broadcasted_iota(jnp.int32, (UNIT, UNIT), 1)
    starts = jnp.sum(jnp.where(before < doc, lens, 0.0), axis=1, keepdims=True)
    unit = [(2 * p + u).astype(F32) for u in range(2)]
    first = [
        jnp.max(jnp.where(starts <= unit[u], starts, 0.0), axis=0, keepdims=True)
        for u in range(2)
    ]

    def token(index):
        jj = index // 16
        return (jj // 2) * 32 + (index % 16) * 2 + jj % 2

    lane = lax.broadcasted_iota(jnp.int32, (UNIT, DIM), 1)
    place = token(lax.broadcasted_iota(jnp.int32, (UNIT, DIM), 0))
    half = DIM // 2
    freq = jnp.exp((lane % half).astype(F32) * (-2.0 * math.log(THETA) / DIM))
    for u in range(2):
        angle = (place.astype(F32) + (unit[u] - first[u]) * UNIT) * freq
        cosw[u * UNIT : (u + 1) * UNIT] = jnp.cos(angle)
        sinw[u * UNIT : (u + 1) * UNIT] = jnp.where(lane < half, -1.0, 1.0) * jnp.sin(angle)

    causal = jnp.where(
        token(lax.broadcasted_iota(jnp.int32, (UNIT, UNIT), 0))
        <= token(lax.broadcasted_iota(jnp.int32, (UNIT, UNIT), 1)),
        0.0,
        MASKED,
    )
    seen = [
        [jnp.where(first[u] <= unit[u] - back, 0.0, MASKED) for back in (2, 1)]
        for u in range(2)
    ]
    qgain = qgain_ref[...].astype(F32)
    kgain = kgain_ref[...].astype(F32)

    def turn(a):
        return a * cosw[...] + swap_halves(a) * sinw[...]

    def turn_back(a):
        return a * cosw[...] - swap_halves(a) * sinw[...]

    def norm(raw):
        wide = raw.astype(F32)
        inv = lax.rsqrt(jnp.mean(wide * wide, axis=1, keepdims=True) + EPS)
        return wide * inv, inv

    def norm_back(grad, hat, inv, gain):
        turned = turn_back(grad)
        scaled = turned * gain
        out = inv * (scaled - hat * jnp.mean(scaled * hat, axis=1, keepdims=True))
        return out.astype(BF16), jnp.sum(turned * hat, axis=0, keepdims=True)

    def spread(n):
        _, _, lane, width = sources[n]
        lanes = pl.ds(lane, width)
        wait(r1.at[:, lanes], sem1.at[n])
        if n + AHEAD < len(sources):
            depart(n + AHEAD)
        moved = dot(perm[...], r1[:, lanes], ((1,), (0,))).astype(BF16)
        s2[:, :, lanes] = moved.reshape(16, 16, width)
        here = r2.at[:, pl.ds(pl.multiple_of(j * 16, 16), 16), lanes]

        def go(i):
            other, device = j_peer(i)
            remote(s2.at[pl.ds(other * 2, 2), :, lanes], here, send.at[1], sem2.at[n], device)

        pltpu.make_async_copy(s2.at[pl.ds(j * 2, 2), :, lanes], here, sem2.at[n]).start()
        each(NJ - 1, go)

    def arrived(n):
        _, _, lane, width = sources[n]
        wait(r2.at[:, :, pl.ds(lane, width)], sem2.at[n])

    def give_back(n, lane, width):
        lanes = pl.ds(lane, width)
        here = r3.at[pl.ds(j * 2, 2), :, lanes]

        def block(other):
            return s3.at[:, pl.ds(pl.multiple_of(other * 16, 16), 16), lanes]

        def go(i):
            other, device = j_peer(i)
            remote(block(other), here, send.at[2], sem3.at[n], device)

        pltpu.make_async_copy(block(j), here, sem3.at[n]).start()
        each(NJ - 1, go)

    def send_home(n, lane, width):
        lanes = pl.ds(lane, width)
        wait(r3.at[:, :, lanes], sem3.at[n])
        moved = dot(perm[...], r3[:, :, lanes].reshape(ROWS, width), ((1,), (0,)))
        s4[:, lanes] = moved.astype(BF16)
        here = back_out.at[pl.ds(pl.multiple_of(z * 16, 16), 16), lanes]

        def block(other):
            return s4.at[pl.ds(pl.multiple_of(other * 16, 16), 16), lanes]

        def go(i):
            other, device = z_peer(i)
            remote(block(other), here, send.at[3], sem4.at[n], device)

        pltpu.make_async_copy(block(z), here, sem4.at[n]).start()
        each(NZ - 1, go)

    following = owner(p + 1)
    preceding = owner(p - 1)

    def window(u):
        return slice(u * UNIT, (u + 3) * UNIT)

    def head(h):
        return slice(h * DIM, (h + 1) * DIM)

    def keys():
        arrived(0)
        hat, inv = norm(r2[:, :, K_AT : K_AT + DIM].reshape(2 * UNIT, DIM))
        khat[...] = hat
        kinv[...] = inv
        kwin[2 * UNIT :] = turn(hat * kgain).astype(BF16)
        remote(kwin.at[pl.ds(2 * UNIT, 2 * UNIT)], kwin.at[pl.ds(0, 2 * UNIT)], send.at[4], semh.at[0], following)
        arrived(1)
        vwin[2 * UNIT :] = r2[:, :, V_AT : V_AT + DIM].reshape(2 * UNIT, DIM)
        remote(vwin.at[pl.ds(2 * UNIT, 2 * UNIT)], vwin.at[pl.ds(0, 2 * UNIT)], send.at[5], semh.at[1], following)
        dkacc[...] = jnp.zeros_like(dkacc)
        dvacc[...] = jnp.zeros_like(dvacc)

    def scores(h):
        arrived(2 + h)
        raw = r2[:, :, Q_AT + h * DIM : Q_AT + (h + 1) * DIM].reshape(2 * UNIT, DIM)
        hat, inv = norm(raw)
        qhat[h] = hat
        qinv[h] = inv
        rot = turn(hat * qgain).astype(BF16)
        for u in range(2):
            qrot[u, head(h)] = rot[u * UNIT : (u + 1) * UNIT]
        if h == 0:
            wait(kwin.at[pl.ds(0, 2 * UNIT)], semh.at[0])
        for u in range(2):
            s = dot(kwin[window(u)], qrot[u, head(h)], ((1,), (1,))) * SCALE
            s = jnp.concatenate(
                [
                    s[:UNIT] + seen[u][0],
                    s[UNIT : 2 * UNIT] + seen[u][1],
                    s[2 * UNIT :] + causal,
                ],
                axis=0,
            )
            e = jnp.exp(s - jnp.max(s, axis=0, keepdims=True))
            prob[u, h] = e * (1.0 / jnp.sum(e, axis=0, keepdims=True))

    def gradients(h):
        arrived(2 + HEADS + h)
        if h == 0:
            wait(vwin.at[pl.ds(0, 2 * UNIT)], semh.at[1])
        grads = []
        for u in range(2):
            g = r2[u, :, G_AT + h * DIM : G_AT + (h + 1) * DIM]
            att = prob[u, h]
            low = att.astype(BF16)
            datt = dot(vwin[window(u)], g, ((1,), (1,)))
            delta = jnp.sum(low.astype(F32) * datt, axis=0, keepdims=True)
            ds = (att * (datt - delta)).astype(BF16)
            dvacc[window(u)] += dot(low, g, ((1,), (0,)))
            dkacc[window(u)] += dot(ds, qrot[u, head(h)], ((1,), (0,)))
            dq = dot(ds, kwin[window(u)], ((0,), (0,))) * SCALE
            grads.append(dq.astype(BF16).astype(F32))
        if h == HEADS - 1:
            halo_s[0] = dvacc[: 2 * UNIT].astype(BF16)
            halo_s[1] = (dkacc[: 2 * UNIT] * SCALE).astype(BF16)
            remote(halo_s, halo_r, send.at[6], semh.at[2], preceding)
        out, part = norm_back(jnp.concatenate(grads, axis=0), qhat[h], qinv[h], qgain)
        s3[:, :, DQ_AT + h * DIM : DQ_AT + (h + 1) * DIM] = out.reshape(2, UNIT, DIM)
        give_back(h, DQ_AT + h * DIM, DIM)
        return part

    which = lax.broadcasted_iota(jnp.int32, (8, DIM), 0)

    def share(stage, value, slots, mine, count, peer):
        gpart[stage] = value
        slots[mine] = value

        def go(i):
            remote(gpart.at[stage], slots.at[mine], send.at[7 + stage], semg.at[stage], peer(i)[1])

        each(count - 1, go)

    def total(stage, slots, count):
        wait(slots.at[pl.ds(0, count - 1)], semg.at[stage])
        return jnp.sum(slots[...], axis=0)

    q_at, g_at = 2, 2 + HEADS
    spread(0)
    spread(1)
    spread(q_at)
    keys()
    spread(q_at + 1)
    spread(q_at + 2)
    scores(0)
    spread(q_at + 3)
    scores(1)
    spread(g_at)
    scores(2)
    spread(g_at + 1)
    scores(3)
    qpart = gradients(0)
    spread(g_at + 2)
    qpart += gradients(1)
    spread(g_at + 3)
    send_home(0, DQ_AT, DIM)
    qpart += gradients(2)
    send_home(1, DQ_AT + DIM, DIM)
    qpart += gradients(3)
    send_home(2, DQ_AT + 2 * DIM, DIM)

    wait(halo_r, semh.at[2])
    dk = dkacc[2 * UNIT :] * SCALE + halo_r[1].astype(F32)
    out, kpart = norm_back(dk.astype(BF16).astype(F32), khat[...], kinv[...], kgain)
    s3[:, :, DK_AT:DV_AT] = out.reshape(2, UNIT, DIM)
    give_back(HEADS, DK_AT, DIM)
    dv = dvacc[2 * UNIT :] + halo_r[0].astype(F32)
    s3[:, :, DV_AT:] = dv.astype(BF16).reshape(2, UNIT, DIM)
    give_back(HEADS + 1, DV_AT, DIM)
    own = jnp.where(which == 0, qpart, jnp.where(which == 1, kpart, 0.0))
    share(0, own, gx, x, NX, x_peer)
    send_home(3, DQ_AT + 3 * DIM, DIM)
    share(1, total(0, gx, NX), gj, j, NJ, j_peer)
    send_home(HEADS, DK_AT, DIM)
    send_home(HEADS + 1, DV_AT, DIM)
    share(2, total(1, gj, NJ), gz, z, NZ, z_peer)
    gain_out[...] = total(2, gz, NZ)

    for n in range(HEADS + 2):
        wait(back_out.at[:, pl.ds(n * DIM, DIM)], sem4.at[n])

    wait(r1.at[pl.ds(0, ROWS - 16)], send.at[0])
    wait(s2.at[pl.ds(0, 16 - 2)], send.at[1])
    wait(s3.at[:, pl.ds(0, UNIT - 16)], send.at[2])
    wait(s4.at[pl.ds(0, ROWS - 16)], send.at[3])
    wait(kwin.at[pl.ds(0, 2 * UNIT)], send.at[4])
    wait(vwin.at[pl.ds(0, 2 * UNIT)], send.at[5])
    wait(halo_s, send.at[6])
    wait(gx.at[pl.ds(0, NX - 1)], send.at[7])
    wait(gj.at[pl.ds(0, NJ - 1)], send.at[8])
    wait(gz.at[pl.ds(0, NZ - 1)], send.at[9])


def local(query_pre, key_pre, values, grad_out, query_gain, key_gain, doc_units):
    vmem = pl.BlockSpec(memory_space=pltpu.VMEM)
    dma = pltpu.SemaphoreType.DMA
    back, gains = pl.pallas_call(
        kernel,
        out_shape=[
            jax.ShapeDtypeStruct((ROWS, BACK), BF16),
            jax.ShapeDtypeStruct((8, DIM), F32),
        ],
        in_specs=[pl.BlockSpec(memory_space=pltpu.HBM)] * 7,
        out_specs=[vmem] * 2,
        scratch_shapes=[
            pltpu.VMEM((1, DIM), BF16),
            pltpu.VMEM((1, DIM), BF16),
            pltpu.VMEM((1, UNIT), jnp.int32),
            pltpu.VMEM((ROWS, FWD), BF16),
            pltpu.VMEM((16, 16, FWD), BF16),
            pltpu.VMEM((2, UNIT, FWD), BF16),
            pltpu.VMEM((2, UNIT, BACK), BF16),
            pltpu.VMEM((16, 16, BACK), BF16),
            pltpu.VMEM((ROWS, BACK), BF16),
            pltpu.VMEM((4 * UNIT, DIM), BF16),
            pltpu.VMEM((4 * UNIT, DIM), BF16),
            pltpu.VMEM((2, 2 * UNIT, DIM), BF16),
            pltpu.VMEM((2, 2 * UNIT, DIM), BF16),
            pltpu.VMEM((2, HEADS * UNIT, DIM), BF16),
            pltpu.VMEM((HEADS, 2 * UNIT, DIM), F32),
            pltpu.VMEM((HEADS, 2 * UNIT, 1), F32),
            pltpu.VMEM((2 * UNIT, DIM), F32),
            pltpu.VMEM((2 * UNIT, 1), F32),
            pltpu.VMEM((2, HEADS, 3 * UNIT, UNIT), F32),
            pltpu.VMEM((4 * UNIT, DIM), F32),
            pltpu.VMEM((4 * UNIT, DIM), F32),
            pltpu.VMEM((ROWS, ROWS), BF16),
            pltpu.VMEM((2 * UNIT, DIM), F32),
            pltpu.VMEM((2 * UNIT, DIM), F32),
            pltpu.VMEM((3, 8, DIM), F32),
            pltpu.VMEM((NX, 8, DIM), F32),
            pltpu.VMEM((NJ, 8, DIM), F32),
            pltpu.VMEM((NZ, 8, DIM), F32),
            dma((2 + 2 * HEADS,)),
            dma((2 + 2 * HEADS,)),
            dma((2 + HEADS,)),
            dma((2 + HEADS,)),
            dma((3,)),
            dma((3,)),
            dma((10,)),
            dma((3,)),
        ],
        compiler_params=pltpu.CompilerParams(
            collective_id=0, has_side_effects=True, vmem_limit_bytes=63 * 1024 * 1024
        ),
        cost_estimate=pl.CostEstimate(
            flops=1_300_000_000, bytes_accessed=4_000_000, transcendentals=1_000_000
        ),
    )(
        query_pre[:, 0, :],
        key_pre[:, 0, :],
        values[:, 0, :],
        grad_out[:, 0, :],
        query_gain.reshape(1, DIM),
        key_gain.reshape(1, DIM),
        doc_units.reshape(1, UNIT),
    )
    back = back[:, None, :]
    return back[..., :DK_AT], back[..., DK_AT:DV_AT], back[..., DV_AT:], gains[0], gains[1]


def solution(mesh):
    token = P(None, "dc", "tp")
    return jax.shard_map(
        local,
        mesh=mesh,
        in_specs=(token, token, token, token, P(), P(), P()),
        out_specs=(token, token, token, P(), P()),
        check_vma=False,
    )
```

time: 98.6 us -> 86 us (0.87)
  Pallas kernels: 91 us -> 80.2 us
  local copies, waits for them, and re-layouts: 6.72 us -> 4.48 us
    pallas_call x1, Pallas kernels: 91 us -> 80.2 us  [local(): pl.pallas_call(kernel, out_shape=[jax.ShapeDtypeStruct((ROWS, BACK), BF16...]
    unnamed x17 -> x0, local copies, waits for them, and re-layouts: 6.2 us -> none
    slice x0 -> x2, local copies, waits for them, and re-layouts: none -> 3.2 us  [the longest x1 1.67 us: local(): back[..., :DK_AT]]
where the time goes in v1:
time: 86 us; the launch traced here: 85.3 us
  Pallas kernels  80.2 us (93%)
  local copies, waits for them, and re-layouts  4.48 us (5%)
    pallas_call x1, Pallas kernels, local(): pl.pallas_call(kernel, out_shape=[jax.ShapeDtypeStruct((ROWS, BACK), BF16...  80.2 us

profile of v1, /device:TPU:1, one launch (start us, length us, event | category | flops | bytes accessed | tf_op | source)
XLA Modules:
  0.0 85.3 jit_solution(1135464795266219269)
XLA Ops:
  0.6 80.2 %shard_map.110 = (bf16[256,768]{1,0:T(8,128)(2,1)}, f32[8,128]{1,0:T(8,128)}) custom-call(bf16[256,512]{1,0:T(8,128)(2,1)} %bitcast.14, bf16[256,128]{1,0:T(8,128)(2,1)} %bitcast.16, bf16[256,128]{1,0:T(8,128)(2,1)} %bitcast.17, bf16[256,512]{1,0:T(8,128)(2,1)} %bitcast.15, bf16[1,128]{1,0:T(2,128)(2,1)} %bitcast.18, bf16[1,128]{1,0:T(2,128)(2,1)} %bitcast.19, ...), custom_call_target="tpu_custom_call" | custom-call | flops 1300000000 | bytes 4000000 | tf_op jit(solution)/shard_map/pallas_call | solution.py:390
  80.8 1.3 %slice_bitcast_fusion = (f32[128]{0:T(128)}, f32[128]{0:T(128)}) fusion(f32[8,128]{1,0:T(8,128)} %get-tuple-element.8), kind=kLoop, calls=%fused_computation | loop fusion | bytes 2048 | tf_op jit(solution)/shard_map/squeeze | solution.py:452
  82.1 1.5 %fusion = (bf16[256,1,128]{2,0,1:T(8,128)(2,1)}, bf16[256,1,128]{2,0,1:T(8,128)(2,1)}) fusion(bf16[256,1,768]{2,0,1:T(8,128)(2,1)} %bitcast.12), kind=kLoop, calls=%fused_computation.2 | loop fusion | bytes 262144 | tf_op jit(solution)/shard_map/slice | solution.py:452
  83.7 1.7 %slice.20 = bf16[256,1,512]{2,0,1:T(8,128)(2,1)} slice(bf16[256,1,768]{2,0,1:T(8,128)(2,1)} %bitcast.13), slice={[0:256], [0:1], [0:512]} | slice | bytes 524288 | tf_op jit(solution)/shard_map/slice | solution.py:452

commit v2 on v1

--- a/solution.py
+++ b/solution.py
@@ -23,6 +23,7 @@
 
 K_AT, V_AT, Q_AT, G_AT, FWD = 0, 128, 256, 768, 1280
 DQ_AT, DK_AT, DV_AT, BACK = 0, 512, 640, 768
+HALO = 256
 
 MESH = pl.DeviceIdType.MESH
 F32 = jnp.float32
@@ -41,8 +42,9 @@
     q_in, k_in, v_in, g_in, qgain_in, kgain_in, docs_in,
     back_out, gain_out,
     qgain_ref, kgain_ref, docs_ref,
-    r1, s2, r2, s3, r3, s4, kwin, vwin, halo_s, halo_r,
-    qrot, qhat, qinv, khat, kinv, prob, dkacc, dvacc, perm, cosw, sinw, gpart,
+    r1, s2, r2, s3, r3, s4, kraw, vraw, h3, hr3, kwin, vwin,
+    qrot, qhat, qinv, khat, prob, dkacc, dvacc, perm, cosw, sinw, gpart,
+    home_k, home_hat, home_inv, home_cos, home_sin,
     gx, gj, gz,
     sem1, sem2, sem3, sem4, semh, semg, send, small,
 ):
@@ -93,7 +95,7 @@
         pltpu.make_async_copy(ref, ref, sem).wait()
 
     for n, (src, dst) in enumerate(
-        ((qgain_in, qgain_ref), (kgain_in, kgain_ref), (docs_in, docs_ref))
+        ((qgain_in, qgain_ref), (kgain_in, kgain_ref), (docs_in, docs_ref), (k_in, home_k))
     ):
         pltpu.make_async_copy(src, dst, small.at[n]).start()
     barrier = pltpu.get_barrier_semaphore()
@@ -106,7 +108,13 @@
     each(NX - 1, lambda i: greet(x_peer(i)[1]))
     greet(owner(p + 1))
     greet(owner(p - 1))
-    pl.semaphore_wait(barrier, NZ - 1 + NJ - 1 + NX - 1 + 2)
+
+    @pl.when(j != 0)
+    def _():
+        greet(at(0, (z + 1) & (NZ - 1), 0))
+
+    greeted = NZ - 1 + NJ - 1 + NX - 1 + 2
+    pl.semaphore_wait(barrier, jnp.where(j == 0, greeted + NJ - 1, greeted))
 
     sources = [(k_in, 0, K_AT, DIM), (v_in, 0, V_AT, DIM)]
     sources += [(q_in, h * DIM, Q_AT + h * DIM, DIM) for h in range(HEADS)]
@@ -136,6 +144,7 @@
     wait(qgain_ref, small.at[0])
     wait(kgain_ref, small.at[1])
     wait(docs_ref, small.at[2])
+    wait(home_k, small.at[3])
 
     lens = jnp.broadcast_to(docs_ref[...].astype(F32), (UNIT, UNIT))
     doc = lax.broadcasted_iota(jnp.int32, (UNIT, UNIT), 0)
@@ -155,10 +164,22 @@
     place = token(lax.broadcasted_iota(jnp.int32, (UNIT, DIM), 0))
     half = DIM // 2
     freq = jnp.exp((lane % half).astype(F32) * (-2.0 * math.log(THETA) / DIM))
-    for u in range(2):
-        angle = (place.astype(F32) + (unit[u] - first[u]) * UNIT) * freq
-        cosw[u * UNIT : (u + 1) * UNIT] = jnp.cos(angle)
-        sinw[u * UNIT : (u + 1) * UNIT] = jnp.where(lane < half, -1.0, 1.0) * jnp.sin(angle)
+    sign = jnp.where(lane < half, -1.0, 1.0)
+    for w in range(4):
+        angle = (place.astype(F32) + (unit[0] + (w - 2.0) - first[w // 3]) * UNIT) * freq
+        cosw[w * UNIT : (w + 1) * UNIT] = jnp.cos(angle)
+        sinw[w * UNIT : (w + 1) * UNIT] = sign * jnp.sin(angle)
+
+    col = lax.broadcasted_iota(jnp.int32, (UNIT, UNIT), 1)
+    upper = jnp.where(doc < col, 1.0, 0.0).astype(BF16)
+    starts_row = dot(lens[:8].astype(BF16), upper, ((1,), (0,)))[:1]
+    for half_rows in range(2):
+        here = slice(half_rows * UNIT, (half_rows + 1) * UNIT)
+        units = (doc + half_rows * UNIT).astype(F32)
+        begun = jnp.max(jnp.where(starts_row <= units, starts_row, 0.0), axis=1, keepdims=True)
+        angle = ((units - begun) * UNIT + me.astype(F32)) * freq
+        home_cos[here] = jnp.cos(angle)
+        home_sin[here] = sign * jnp.sin(angle)
 
     causal = jnp.where(
         token(lax.broadcasted_iota(jnp.int32, (UNIT, UNIT), 0))
@@ -173,22 +194,22 @@
     qgain = qgain_ref[...].astype(F32)
     kgain = kgain_ref[...].astype(F32)
 
-    def turn(a):
-        return a * cosw[...] + swap_halves(a) * sinw[...]
-
-    def turn_back(a):
-        return a * cosw[...] - swap_halves(a) * sinw[...]
+    def turn(a, cos, sin):
+        return a * cos + swap_halves(a) * sin
 
     def norm(raw):
         wide = raw.astype(F32)
         inv = lax.rsqrt(jnp.mean(wide * wide, axis=1, keepdims=True) + EPS)
         return wide * inv, inv
 
-    def norm_back(grad, hat, inv, gain):
-        turned = turn_back(grad)
+    def norm_back(turned, hat, inv, gain):
         scaled = turned * gain
         out = inv * (scaled - hat * jnp.mean(scaled * hat, axis=1, keepdims=True))
-        return out.astype(BF16), jnp.sum(turned * hat, axis=0, keepdims=True)
+        return out.astype(BF16)
+
+    home_hat[...], home_inv[...] = norm(home_k[...])
+    own_rows = slice(2 * UNIT, 4 * UNIT)
+    own_cos, own_sin = cosw[own_rows], sinw[own_rows]
 
     def spread(n):
         _, _, lane, width = sources[n]
@@ -225,11 +246,52 @@
         pltpu.make_async_copy(block(j), here, sem3.at[n]).start()
         each(NJ - 1, go)
 
+    def give_keys_back():
+        lanes = pl.ds(DK_AT, HALO)
+        here = r3.at[pl.ds(j * 2, 2), :, lanes]
+        before = (j + NJ - 1) & (NJ - 1)
+        there = hr3.at[pl.ds(before * 2, 2)]
+        row = jnp.where(j == 0, z + NZ - 1, z) & (NZ - 1)
+
+        def block(ref, other, width):
+            return ref.at[:, pl.ds(pl.multiple_of(other * 16, 16), 16), width]
+
+        def go(i):
+            other, device = j_peer(i)
+            remote(block(s3, other, lanes), here, send.at[2], sem3.at[HEADS], device)
+            remote(block(h3, other, pl.ds(0, HALO)), there, send.at[5], sem3.at[HEADS + 1], at(other // 2, row, other & 1))
+
+        pltpu.make_async_copy(block(s3, j, lanes), here, sem3.at[HEADS]).start()
+        own = block(h3, j, pl.ds(0, HALO))
+
+        @pl.when(j == 0)
+        def _():
+            remote(own, there, send.at[6], sem3.at[HEADS + 1], at(y, row, c))
+
+        @pl.when(j != 0)
+        def _():
+            pltpu.make_async_copy(own, there, sem3.at[HEADS + 1]).start()
+
+        each(NJ - 1, go)
+
+    def keys_home():
+        wait(r3.at[:, :, pl.ds(DK_AT, HALO)], sem3.at[HEADS])
+        wait(hr3, sem3.at[HEADS + 1])
+        total = dot(perm[...], r3[:, :, DK_AT:].reshape(ROWS, HALO), ((1,), (0,)))
+        total += dot(perm[...], hr3[...].reshape(ROWS, HALO), ((1,), (0,)))
+        s4[:, DK_AT:] = total.astype(BF16)
+        along_z(HEADS, DK_AT, DIM)
+        along_z(HEADS + 1, DV_AT, DIM)
+
     def send_home(n, lane, width):
         lanes = pl.ds(lane, width)
         wait(r3.at[:, :, lanes], sem3.at[n])
         moved = dot(perm[...], r3[:, :, lanes].reshape(ROWS, width), ((1,), (0,)))
         s4[:, lanes] = moved.astype(BF16)
+        along_z(n, lane, width)
+
+    def along_z(n, lane, width):
+        lanes = pl.ds(lane, width)
         here = back_out.at[pl.ds(pl.multiple_of(z * 16, 16), 16), lanes]
 
         def block(other):
@@ -243,7 +305,6 @@
         each(NZ - 1, go)
 
     following = owner(p + 1)
-    preceding = owner(p - 1)
 
     def window(u):
         return slice(u * UNIT, (u + 3) * UNIT)
@@ -253,16 +314,20 @@
 
     def keys():
         arrived(0)
-        hat, inv = norm(r2[:, :, K_AT : K_AT + DIM].reshape(2 * UNIT, DIM))
-        khat[...] = hat
-        kinv[...] = inv
-        kwin[2 * UNIT :] = turn(hat * kgain).astype(BF16)
-        remote(kwin.at[pl.ds(2 * UNIT, 2 * UNIT)], kwin.at[pl.ds(0, 2 * UNIT)], send.at[4], semh.at[0], following)
+        k_here = r2.at[:, :, pl.ds(K_AT, DIM)]
+        remote(k_here, kraw, send.at[4], semh.at[0], following)
         arrived(1)
-        vwin[2 * UNIT :] = r2[:, :, V_AT : V_AT + DIM].reshape(2 * UNIT, DIM)
-        remote(vwin.at[pl.ds(2 * UNIT, 2 * UNIT)], vwin.at[pl.ds(0, 2 * UNIT)], send.at[5], semh.at[1], following)
+        v_here = r2.at[:, :, pl.ds(V_AT, DIM)]
+        remote(v_here, vraw, send.at[7], semh.at[1], following)
+        use_keys(k_here[...], own_rows)
+        vwin[own_rows] = v_here[...].reshape(2 * UNIT, DIM)
         dkacc[...] = jnp.zeros_like(dkacc)
         dvacc[...] = jnp.zeros_like(dvacc)
+
+    def use_keys(raw, rows):
+        hat, _ = norm(raw.reshape(2 * UNIT, DIM))
+        khat[rows] = hat
+        kwin[rows] = turn(hat * kgain, cosw[rows], sinw[rows]).astype(BF16)
 
     def scores(h):
         arrived(2 + h)
@@ -270,11 +335,12 @@
         hat, inv = norm(raw)
         qhat[h] = hat
         qinv[h] = inv
-        rot = turn(hat * qgain).astype(BF16)
+        rot = turn(hat * qgain, own_cos, own_sin).astype(BF16)
         for u in range(2):
             qrot[u, head(h)] = rot[u * UNIT : (u + 1) * UNIT]
         if h == 0:
-            wait(kwin.at[pl.ds(0, 2 * UNIT)], semh.at[0])
+            wait(kraw, semh.at[0])
+            use_keys(kraw[...], slice(0, 2 * UNIT))
         for u in range(2):
             s = dot(kwin[window(u)], qrot[u, head(h)], ((1,), (1,))) * SCALE
             s = jnp.concatenate(
@@ -291,7 +357,8 @@
     def gradients(h):
         arrived(2 + HEADS + h)
         if h == 0:
-            wait(vwin.at[pl.ds(0, 2 * UNIT)], semh.at[1])
+            wait(vraw, semh.at[1])
+            vwin[: 2 * UNIT] = vraw[...].reshape(2 * UNIT, DIM)
         grads = []
         for u in range(2):
             g = r2[u, :, G_AT + h * DIM : G_AT + (h + 1) * DIM]
@@ -304,23 +371,30 @@
             dkacc[window(u)] += dot(ds, qrot[u, head(h)], ((1,), (0,)))
             dq = dot(ds, kwin[window(u)], ((0,), (0,))) * SCALE
             grads.append(dq.astype(BF16).astype(F32))
-        if h == HEADS - 1:
-            halo_s[0] = dvacc[: 2 * UNIT].astype(BF16)
-            halo_s[1] = (dkacc[: 2 * UNIT] * SCALE).astype(BF16)
-            remote(halo_s, halo_r, send.at[6], semh.at[2], preceding)
-        out, part = norm_back(jnp.concatenate(grads, axis=0), qhat[h], qinv[h], qgain)
+        turned = turn(jnp.concatenate(grads, axis=0), own_cos, -own_sin)
+        out = norm_back(turned, qhat[h], qinv[h], qgain)
         s3[:, :, DQ_AT + h * DIM : DQ_AT + (h + 1) * DIM] = out.reshape(2, UNIT, DIM)
         give_back(h, DQ_AT + h * DIM, DIM)
-        return part
-
-    which = lax.broadcasted_iota(jnp.int32, (8, DIM), 0)
+        if h == HEADS - 1:
+            dk = dkacc[...] * SCALE
+            low = dk.astype(BF16).reshape(4, UNIT, DIM)
+            s3[:, :, DK_AT:DV_AT] = low[2:]
+            h3[:, :, :DIM] = low[:2]
+            low = dvacc[...].astype(BF16).reshape(4, UNIT, DIM)
+            s3[:, :, DV_AT:] = low[2:]
+            h3[:, :, DIM:] = low[:2]
+            give_keys_back()
+            turned_k = turn(dk, cosw[...], -sinw[...])
+            gpart[0, 1:2] = jnp.sum(turned_k * khat[...], axis=0, keepdims=True)
+        return jnp.sum(turned * qhat[h], axis=0, keepdims=True)
 
     def share(stage, value, slots, mine, count, peer):
-        gpart[stage] = value
-        slots[mine] = value
+        if value is not None:
+            gpart[stage] = value
+        slots[mine] = gpart[stage]
 
         def go(i):
-            remote(gpart.at[stage], slots.at[mine], send.at[7 + stage], semg.at[stage], peer(i)[1])
+            remote(gpart.at[stage], slots.at[mine], send.at[8 + stage], semg.at[stage], peer(i)[1])
 
         each(count - 1, go)
 
@@ -350,38 +424,58 @@
     qpart += gradients(2)
     send_home(1, DQ_AT + DIM, DIM)
     qpart += gradients(3)
+    gpart[0, 0:1] = qpart
+    share(0, None, gx, x, NX, x_peer)
     send_home(2, DQ_AT + 2 * DIM, DIM)
-
-    wait(halo_r, semh.at[2])
-    dk = dkacc[2 * UNIT :] * SCALE + halo_r[1].astype(F32)
-    out, kpart = norm_back(dk.astype(BF16).astype(F32), khat[...], kinv[...], kgain)
-    s3[:, :, DK_AT:DV_AT] = out.reshape(2, UNIT, DIM)
-    give_back(HEADS, DK_AT, DIM)
-    dv = dvacc[2 * UNIT :] + halo_r[0].astype(F32)
-    s3[:, :, DV_AT:] = dv.astype(BF16).reshape(2, UNIT, DIM)
-    give_back(HEADS + 1, DV_AT, DIM)
-    own = jnp.where(which == 0, qpart, jnp.where(which == 1, kpart, 0.0))
-    share(0, own, gx, x, NX, x_peer)
+    share(1, total(0, gx, NX), gj, j, NJ, j_peer)
     send_home(3, DQ_AT + 3 * DIM, DIM)
-    share(1, total(0, gx, NX), gj, j, NJ, j_peer)
-    send_home(HEADS, DK_AT, DIM)
-    send_home(HEADS + 1, DV_AT, DIM)
     share(2, total(1, gj, NJ), gz, z, NZ, z_peer)
+    keys_home()
+    for n in range(HEADS + 1):
+        wait(back_out.at[:, pl.ds(n * DIM, DIM)], sem4.at[n])
+    dk = turn(back_out[:, DK_AT:DV_AT].astype(F32), home_cos[...], -home_sin[...])
+    back_out[:, DK_AT:DV_AT] = norm_back(dk, home_hat[...], home_inv[...], kgain)
     gain_out[...] = total(2, gz, NZ)
-
-    for n in range(HEADS + 2):
-        wait(back_out.at[:, pl.ds(n * DIM, DIM)], sem4.at[n])
+    wait(back_out.at[:, pl.ds(DV_AT, DIM)], sem4.at[HEADS + 1])
 
     wait(r1.at[pl.ds(0, ROWS - 16)], send.at[0])
     wait(s2.at[pl.ds(0, 16 - 2)], send.at[1])
     wait(s3.at[:, pl.ds(0, UNIT - 16)], send.at[2])
     wait(s4.at[pl.ds(0, ROWS - 16)], send.at[3])
-    wait(kwin.at[pl.ds(0, 2 * UNIT)], send.at[4])
-    wait(vwin.at[pl.ds(0, 2 * UNIT)], send.at[5])
-    wait(halo_s, send.at[6])
-    wait(gx.at[pl.ds(0, NX - 1)], send.at[7])
-    wait(gj.at[pl.ds(0, NJ - 1)], send.at[8])
-    wait(gz.at[pl.ds(0, NZ - 1)], send.at[9])
+    wait(kraw, send.at[4])
+    wait(hr3.at[pl.ds(0, 16 - 2)], send.at[5])
+
+    @pl.when(j == 0)
+    def _():
+        wait(hr3.at[pl.ds(0, 2)], send.at[6])
+
+    wait(vraw, send.at[7])
+    wait(gx.at[pl.ds(0, NX - 1)], send.at[8])
+    wait(gj.at[pl.ds(0, NJ - 1)], send.at[9])
+    wait(gz.at[pl.ds(0, NZ - 1)], send.at[10])
+
+
+def finish(back, gains, dq, dk, dv, gain_q, gain_k, held, held_gains, sems):
+    pieces = (
+        (back.at[:, pl.ds(DQ_AT, HEADS * DIM)], held.at[:, pl.ds(DQ_AT, HEADS * DIM)], dq),
+        (back.at[:, pl.ds(DK_AT, DIM)], held.at[:, pl.ds(DK_AT, DIM)], dk),
+        (back.at[:, pl.ds(DV_AT, DIM)], held.at[:, pl.ds(DV_AT, DIM)], dv),
+        (gains.at[pl.ds(0, 1)], held_gains.at[pl.ds(0, 1)], gain_q),
+        (gains.at[pl.ds(1, 1)], held_gains.at[pl.ds(1, 1)], gain_k),
+    )
+    arriving = [
+        pltpu.make_async_copy(src, mid, sems.at[0, n]) for n, (src, mid, _) in enumerate(pieces)
+    ]
+    leaving = [
+        pltpu.make_async_copy(mid, dst, sems.at[1, n]) for n, (_, mid, dst) in enumerate(pieces)
+    ]
+    for copy in arriving:
+        copy.start()
+    for first, second in zip(arriving, leaving):
+        first.wait()
+        second.start()
+    for copy in leaving:
+        copy.wait()
 
 
 def local(query_pre, key_pre, values, grad_out, query_gain, key_gain, doc_units):
@@ -391,7 +485,7 @@
         kernel,
         out_shape=[
             jax.ShapeDtypeStruct((ROWS, BACK), BF16),
-            jax.ShapeDtypeStruct((8, DIM), F32),
+            jax.ShapeDtypeStruct((2, DIM), F32),
         ],
         in_specs=[pl.BlockSpec(memory_space=pltpu.HBM)] * 7,
         out_specs=[vmem] * 2,
@@ -405,33 +499,39 @@
             pltpu.VMEM((2, UNIT, BACK), BF16),
             pltpu.VMEM((16, 16, BACK), BF16),
             pltpu.VMEM((ROWS, BACK), BF16),
+            pltpu.VMEM((2, UNIT, DIM), BF16),
+            pltpu.VMEM((2, UNIT, DIM), BF16),
+            pltpu.VMEM((2, UNIT, HALO), BF16),
+            pltpu.VMEM((16, 16, HALO), BF16),
             pltpu.VMEM((4 * UNIT, DIM), BF16),
             pltpu.VMEM((4 * UNIT, DIM), BF16),
-            pltpu.VMEM((2, 2 * UNIT, DIM), BF16),
-            pltpu.VMEM((2, 2 * UNIT, DIM), BF16),
             pltpu.VMEM((2, HEADS * UNIT, DIM), BF16),
             pltpu.VMEM((HEADS, 2 * UNIT, DIM), F32),
             pltpu.VMEM((HEADS, 2 * UNIT, 1), F32),
-            pltpu.VMEM((2 * UNIT, DIM), F32),
-            pltpu.VMEM((2 * UNIT, 1), F32),
+            pltpu.VMEM((4 * UNIT, DIM), F32),
             pltpu.VMEM((2, HEADS, 3 * UNIT, UNIT), F32),
             pltpu.VMEM((4 * UNIT, DIM), F32),
             pltpu.VMEM((4 * UNIT, DIM), F32),
             pltpu.VMEM((ROWS, ROWS), BF16),
-            pltpu.VMEM((2 * UNIT, DIM), F32),
-            pltpu.VMEM((2 * UNIT, DIM), F32),
-            pltpu.VMEM((3, 8, DIM), F32),
-            pltpu.VMEM((NX, 8, DIM), F32),
-            pltpu.VMEM((NJ, 8, DIM), F32),
-            pltpu.VMEM((NZ, 8, DIM), F32),
+            pltpu.VMEM((4 * UNIT, DIM), F32),
+            pltpu.VMEM((4 * UNIT, DIM), F32),
+            pltpu.VMEM((3, 2, DIM), F32),
+            pltpu.VMEM((ROWS, DIM), BF16),
+            pltpu.VMEM((ROWS, DIM), F32),
+            pltpu.VMEM((ROWS, 1), F32),
+            pltpu.VMEM((ROWS, DIM), F32),
+            pltpu.VMEM((ROWS, DIM), F32),
+            pltpu.VMEM((NX, 2, DIM), F32),
+            pltpu.VMEM((NJ, 2, DIM), F32),
+            pltpu.VMEM((NZ, 2, DIM), F32),
             dma((2 + 2 * HEADS,)),
             dma((2 + 2 * HEADS,)),
             dma((2 + HEADS,)),
             dma((2 + HEADS,)),
+            dma((2,)),
             dma((3,)),
-            dma((3,)),
-            dma((10,)),
-            dma((3,)),
+            dma((11,)),
+            dma((4,)),
         ],
         compiler_params=pltpu.CompilerParams(
             collective_id=0, has_side_effects=True, vmem_limit_bytes=63 * 1024 * 1024
@@ -448,8 +548,21 @@
         key_gain.reshape(1, DIM),
         doc_units.reshape(1, UNIT),
     )
-    back = back[:, None, :]
-    return back[..., :DK_AT], back[..., DK_AT:DV_AT], back[..., DV_AT:], gains[0], gains[1]
+    hbm = pl.BlockSpec(memory_space=pltpu.HBM)
+    dq, dk, dv, gain_q, gain_k = pl.pallas_call(
+        finish,
+        out_shape=[
+            jax.ShapeDtypeStruct((ROWS, HEADS * DIM), BF16),
+            jax.ShapeDtypeStruct((ROWS, DIM), BF16),
+            jax.ShapeDtypeStruct((ROWS, DIM), BF16),
+            jax.ShapeDtypeStruct((1, DIM), F32),
+            jax.ShapeDtypeStruct((1, DIM), F32),
+        ],
+        in_specs=[hbm] * 2,
+        out_specs=[hbm] * 5,
+        scratch_shapes=[pltpu.VMEM((ROWS, BACK), BF16), pltpu.VMEM((2, DIM), F32), dma((2, 5))],
+    )(back, gains)
+    return dq[:, None, :], dk[:, None, :], dv[:, None, :], gain_q[0], gain_k[0]
 
 
 def solution(mesh):

time: 86 us -> 78.3 us (0.910)
  local copies, waits for them, and re-layouts: 4.48 us -> 0 us
  Pallas kernels: 80.2 us -> 77.5 us
    pallas_call x1, Pallas kernels: 80.2 us -> 75.8 us  [local(): pl.pallas_call(kernel, out_shape=[jax.ShapeDtypeStruct((ROWS, BACK), BF16...]
    slice x2 -> x0, local copies, waits for them, and re-layouts: 3.2 us -> none  [the longest x1 1.67 us: local(): back[..., :DK_AT]]
    pallas_call x0 -> x1, Pallas kernels: none -> 1.78 us  [local(): pl.pallas_call(finish, out_shape=[jax.ShapeDtypeStruct((ROWS, HEADS * DIM...]
    squeeze x1 -> x0, local copies, waits for them, and re-layouts: 1.28 us -> none  [local(): gains[1]]
where the time goes in v2:
time: 78.3 us; the launch traced here: 78.2 us
  Pallas kernels  77.5 us (99%)
    pallas_call x1, Pallas kernels, local(): pl.pallas_call(kernel, out_shape=[jax.ShapeDtypeStruct((ROWS, BACK), BF16...  75.8 us
    pallas_call x1, Pallas kernels, local(): pl.pallas_call(finish, out_shape=[jax.ShapeDtypeStruct((ROWS, HEADS * DIM...  1.78 us

profile of v2, /device:TPU:1, one launch (start us, length us, event | category | flops | bytes accessed | tf_op | source)
XLA Modules:
  0.0 78.2 jit_solution(114597020335429787)
XLA Ops:
  0.6 75.8 %shard_map.110 = (bf16[256,768]{1,0:T(8,128)(2,1)}, f32[2,128]{1,0:T(2,128)}) custom-call(bf16[256,512]{1,0:T(8,128)(2,1)} %bitcast.12, bf16[256,128]{1,0:T(8,128)(2,1)} %bitcast.15, bf16[256,128]{1,0:T(8,128)(2,1)} %bitcast.16, bf16[256,512]{1,0:T(8,128)(2,1)} %bitcast.13, bf16[1,128]{1,0:T(2,128)(2,1)} %bitcast.19, bf16[1,128]{1,0:T(2,128)(2,1)} %bitcast.20, ...), custom_call_target="tpu_custom_call" | custom-call | flops 1300000000 | bytes 4000000 | tf_op jit(solution)/shard_map/pallas_call | solution.py:484
  76.4 1.8 %shard_map.111 = (bf16[256,512]{1,0:T(8,128)(2,1)}, bf16[256,128]{1,0:T(8,128)(2,1)}, bf16[256,128]{1,0:T(8,128)(2,1)}, f32[1,128]{1,0:T(1,128)}, f32[1,128]{1,0:T(1,128)}) custom-call(bf16[256,768]{1,0:T(8,128)(2,1)} %get-tuple-element.12.back, f32[2,128]{1,0:T(2,128)} %get-tuple-element.13.gains), custom_call_target="tpu_custom_call" | custom-call | tf_op jit(solution)/shard_map/pallas_call | solution.py:552

commit v3 on v2

--- a/solution.py
+++ b/solution.py
@@ -83,7 +83,7 @@
             body(i)
             return carry
 
-        lax.fori_loop(0, count, step, 0)
+        lax.fori_loop(0, count, step, 0, unroll=True)
 
     def remote(src, dst, send_sem, recv_sem, device):
         pltpu.make_async_remote_copy(
@@ -117,7 +117,7 @@
     pl.semaphore_wait(barrier, jnp.where(j == 0, greeted + NJ - 1, greeted))
 
     sources = [(k_in, 0, K_AT, DIM), (v_in, 0, V_AT, DIM)]
-    sources += [(q_in, h * DIM, Q_AT + h * DIM, DIM) for h in range(HEADS)]
+    sources += [(q_in, h * DIM, Q_AT + h * DIM, 2 * DIM) for h in (0, 2)]
     sources += [(g_in, h * DIM, G_AT + h * DIM, DIM) for h in range(HEADS)]
 
     def depart(n):
@@ -330,7 +330,8 @@
         kwin[rows] = turn(hat * kgain, cosw[rows], sinw[rows]).astype(BF16)
 
     def scores(h):
-        arrived(2 + h)
+        if h % 2 == 0:
+            arrived(2 + h // 2)
         raw = r2[:, :, Q_AT + h * DIM : Q_AT + (h + 1) * DIM].reshape(2 * UNIT, DIM)
         hat, inv = norm(raw)
         qhat[h] = hat
@@ -355,7 +356,7 @@
             prob[u, h] = e * (1.0 / jnp.sum(e, axis=0, keepdims=True))
 
     def gradients(h):
-        arrived(2 + HEADS + h)
+        arrived(4 + h)
         if h == 0:
             wait(vraw, semh.at[1])
             vwin[: 2 * UNIT] = vraw[...].reshape(2 * UNIT, DIM)
@@ -402,20 +403,18 @@
         wait(slots.at[pl.ds(0, count - 1)], semg.at[stage])
         return jnp.sum(slots[...], axis=0)
 
-    q_at, g_at = 2, 2 + HEADS
+    q_at, g_at = 2, 4
     spread(0)
     spread(1)
     spread(q_at)
     keys()
     spread(q_at + 1)
-    spread(q_at + 2)
     scores(0)
-    spread(q_at + 3)
     scores(1)
     spread(g_at)
     scores(2)
+    scores(3)
     spread(g_at + 1)
-    scores(3)
     qpart = gradients(0)
     spread(g_at + 2)
     qpart += gradients(1)

time: 78.3 us -> 77.4 us (0.989)
  Pallas kernels: 77.5 us -> 76.6 us
    pallas_call x1, Pallas kernels: 75.8 us -> 74.8 us  [local(): pl.pallas_call(kernel, out_shape=[jax.ShapeDtypeStruct((ROWS, BACK), BF16...]
where the time goes in v3:
time: 77.4 us; the launch traced here: 77.2 us
  Pallas kernels  76.6 us (99%)
    pallas_call x1, Pallas kernels, local(): pl.pallas_call(kernel, out_shape=[jax.ShapeDtypeStruct((ROWS, BACK), BF16...  74.8 us
    pallas_call x1, Pallas kernels, local(): pl.pallas_call(finish, out_shape=[jax.ShapeDtypeStruct((ROWS, HEADS * DIM...  1.78 us

profile of v3, /device:TPU:1, one launch (start us, length us, event | category | flops | bytes accessed | tf_op | source)
XLA Modules:
  0.0 77.2 jit_solution(15092093667711618756)
XLA Ops:
  0.6 74.8 %shard_map.110 = (bf16[256,768]{1,0:T(8,128)(2,1)}, f32[2,128]{1,0:T(2,128)}) custom-call(bf16[256,512]{1,0:T(8,128)(2,1)} %bitcast.12, bf16[256,128]{1,0:T(8,128)(2,1)} %bitcast.15, bf16[256,128]{1,0:T(8,128)(2,1)} %bitcast.16, bf16[256,512]{1,0:T(8,128)(2,1)} %bitcast.13, bf16[1,128]{1,0:T(2,128)(2,1)} %bitcast.19, bf16[1,128]{1,0:T(2,128)(2,1)} %bitcast.20, ...), custom_call_target="tpu_custom_call" | custom-call | flops 1300000000 | bytes 4000000 | tf_op jit(solution)/shard_map/pallas_call | solution.py:483
  75.4 1.8 %shard_map.111 = (bf16[256,512]{1,0:T(8,128)(2,1)}, bf16[256,128]{1,0:T(8,128)(2,1)}, bf16[256,128]{1,0:T(8,128)(2,1)}, f32[1,128]{1,0:T(1,128)}, f32[1,128]{1,0:T(1,128)}) custom-call(bf16[256,768]{1,0:T(8,128)(2,1)} %get-tuple-element.12.back, f32[2,128]{1,0:T(2,128)} %get-tuple-element.13.gains), custom_call_target="tpu_custom_call" | custom-call | tf_op jit(solution)/shard_map/pallas_call | solution.py:551

commit v4 on v3

--- a/solution.py
+++ b/solution.py
@@ -66,7 +66,8 @@
         return other, at(y, other, c)
 
     def j_peer(i):
-        other = (j + 1 + i) & (NJ - 1)
+        k = (i + 1) // 2
+        other = jnp.where((i & 1) == 0, j + NJ // 2 + k, j + NJ // 2 - k) & (NJ - 1)
         return other, at(other // 2, z, other & 1)
 
     def x_peer(i):

time: 77.4 us -> 77.1 us (level)
  no operation moved by 1% of the time
where the time goes in v4:
time: 77.1 us; the launch traced here: 76.9 us
  Pallas kernels  76.3 us (99%)
    pallas_call x1, Pallas kernels, local(): pl.pallas_call(kernel, out_shape=[jax.ShapeDtypeStruct((ROWS, BACK), BF16...  74.5 us
    pallas_call x1, Pallas kernels, local(): pl.pallas_call(finish, out_shape=[jax.ShapeDtypeStruct((ROWS, HEADS * DIM...  1.78 us

profile of v4, /device:TPU:1, one launch (start us, length us, event | category | flops | bytes accessed | tf_op | source)
XLA Modules:
  0.0 76.9 jit_solution(1166224208892673128)
XLA Ops:
  0.6 74.5 %shard_map.110 = (bf16[256,768]{1,0:T(8,128)(2,1)}, f32[2,128]{1,0:T(2,128)}) custom-call(bf16[256,512]{1,0:T(8,128)(2,1)} %bitcast.12, bf16[256,128]{1,0:T(8,128)(2,1)} %bitcast.15, bf16[256,128]{1,0:T(8,128)(2,1)} %bitcast.16, bf16[256,512]{1,0:T(8,128)(2,1)} %bitcast.13, bf16[1,128]{1,0:T(2,128)(2,1)} %bitcast.19, bf16[1,128]{1,0:T(2,128)(2,1)} %bitcast.20, ...), custom_call_target="tpu_custom_call" | custom-call | flops 1300000000 | bytes 4000000 | tf_op jit(solution)/shard_map/pallas_call | solution.py:484
  75.2 1.8 %shard_map.111 = (bf16[256,512]{1,0:T(8,128)(2,1)}, bf16[256,128]{1,0:T(8,128)(2,1)}, bf16[256,128]{1,0:T(8,128)(2,1)}, f32[1,128]{1,0:T(1,128)}, f32[1,128]{1,0:T(1,128)}) custom-call(bf16[256,768]{1,0:T(8,128)(2,1)} %get-tuple-element.12.back, f32[2,128]{1,0:T(2,128)} %get-tuple-element.13.gains), custom_call_target="tpu_custom_call" | custom-call | tf_op jit(solution)/shard_map/pallas_call | solution.py:552
